TPU v7x, 32 devices: a whole 2x2x4 slice. The times are simulated.
32 devices in a mesh: lon: 8 (over z, core), lat: 4 (over y, x).
Axes of the slice: x: 2, y: 2, z: 4, core: 2. Of those that a mesh axis runs over, the one named last changes fastest.
Arguments:
- iterate: float32 [127, 4, 1024], P(None, 'lat', 'lon'), may hold values from -200 to 200
- residual: float32 [127, 4, 1024], P(None, 'lat', 'lon'), may hold values from -200 to 200
- direction: float32 [127, 4, 1024], P(None, 'lat', 'lon'), may hold values from -200 to 200
- obs_weight: float32 [127, 4, 1024], P(None, 'lat', 'lon'), may hold values from 0.5 to 5
- vertical: float32 [127, 127], replicated, may hold values from -0.2 to 1.2
- lon_taps: float32 [32, 101], replicated, may hold values from 0 to 1
- lat_taps: float32 [32, 101], replicated, may hold values from 0 to 1
- band_sizes: int32 [32], replicated, may hold values from 1 to 12, 127 in all
Outputs:
- iterate_next: float32 [127, 4, 1024], P(None, 'lat', 'lon')
- residual_next: float32 [127, 4, 1024], P(None, 'lat', 'lon')
- direction_next: float32 [127, 4, 1024], P(None, 'lat', 'lon')
Inputs may be any that keep to these rules, and one draw needn't show every extreme that they name: `band_sizes`: the bands sum to 127 levels and the largest holds exactly 12 levels.
All inputs are finite; a program needn't handle non-finite values.
Results may differ from a plain program's by a relative error of at most 0.000071.
Values sent between devices are 32-bit elements; how exact they have to be, the bound alone decides.
A program may use at most 64 MiB of HBM per device.

v0:
```python
import jax
import jax.numpy as jnp
from jax import lax
from jax.sharding import PartitionSpec as P

LEV = 127
TAPS = 101
HALF = 50
GROUPS = 32


HIGHEST = lax.Precision.HIGHEST


def with_halo(cells, sides, width):
    for axis, dim in sides:
        count = lax.axis_size(axis)
        head = lax.slice_in_dim(cells, 0, width, axis=dim)
        tail = lax.slice_in_dim(cells, cells.shape[dim] - width, cells.shape[dim], axis=dim)
        cells = jnp.concatenate(
            [
                lax.ppermute(tail, axis, [(i, (i + 1) % count) for i in range(count)]),
                cells,
                lax.ppermute(head, axis, [((i + 1) % count, i) for i in range(count)]),
            ],
            axis=dim,
        )
    return cells


def band_matrices(kernel, width_in, width_out):
    offsets = (
        jnp.arange(width_in, dtype=jnp.int32)[:, None]
        - jnp.arange(width_out, dtype=jnp.int32)[None, :]
        + HALF
    )
    inside = (offsets >= 0) & (offsets < TAPS)
    picked = kernel[:, jnp.clip(offsets, 0, TAPS - 1)]
    return jnp.where(inside[None], picked, jnp.zeros_like(picked))


def group_rows(group_ids, kernel):
    onehot = (group_ids[:, None] == jnp.arange(GROUPS, dtype=jnp.int32)[None, :]).astype(
        jnp.float32
    )
    return jnp.dot(onehot, kernel, precision=HIGHEST)


def slot_plan(groups, devices_count):
    levels = jnp.arange(LEV, dtype=jnp.int32)
    capacity = (LEV + devices_count - 1) // devices_count
    slot_ids = jnp.arange(devices_count * capacity, dtype=jnp.int32)
    matched = levels[None, :] == slot_ids[:, None]
    occupied = jnp.any(matched, axis=1)
    sources = jnp.sum(jnp.where(matched, levels[None, :], 0), axis=1)
    sources = jnp.where(occupied, sources, LEV)
    slot_groups = jnp.sum(jnp.where(matched, groups[None, :], 0), axis=1)
    return (capacity, levels, sources, slot_groups)


def into_slots(grid_field, sources):
    padded = jnp.concatenate(
        [grid_field, jnp.zeros((1,) + grid_field.shape[1:], grid_field.dtype)], axis=0
    )
    return jnp.take(padded, sources, axis=0)


def lon_pass(grid_field, kernel_groups, groups, adjoint):
    kernel = kernel_groups[:, ::-1] if adjoint else kernel_groups
    lon_width = grid_field.shape[2]
    kernels = group_rows(groups, kernel)
    extended = with_halo(grid_field, (("lon", 2),), HALF)
    windows = jnp.stack(
        [extended[:, :, shift_tap : shift_tap + lon_width] for shift_tap in range(TAPS)], axis=2
    )
    return jnp.einsum("lakb,lk->lab", windows, kernels, precision=HIGHEST)


def lat_pass(grid_field, kernel_groups, groups, adjoint):
    kernel = kernel_groups[:, ::-1] if adjoint else kernel_groups
    devices_count = lax.axis_size("lat")
    capacity, position, sources, slot_groups = slot_plan(groups, devices_count)
    slotted = into_slots(grid_field, sources)
    own_groups = lax.dynamic_slice_in_dim(slot_groups, lax.axis_index("lat") * capacity, capacity)
    lat_width = grid_field.shape[1] * devices_count
    matrices = band_matrices(group_rows(own_groups, kernel), lat_width, lat_width)
    filtered = jnp.einsum(
        "sco,scx->sox",
        matrices,
        lax.all_to_all(slotted, "lat", split_axis=0, concat_axis=1, tiled=True),
        precision=HIGHEST,
    )
    returned = lax.all_to_all(filtered, "lat", split_axis=1, concat_axis=0, tiled=True)
    return jnp.take(returned, position, axis=0)


def vertical_mix(matrix, grid_field):
    return jnp.dot(matrix, grid_field.reshape(LEV, -1), precision=HIGHEST).reshape(grid_field.shape)


def local(iterate, residual, direction, obs_weight, vertical, lon_taps, lat_taps, band_sizes):
    bounds = jnp.cumsum(band_sizes)
    levels = jnp.arange(LEV, dtype=jnp.int32)
    groups = jnp.sum((levels[:, None] >= bounds[None, :]).astype(jnp.int32), axis=1)
    lon_part = lon_pass(direction, lon_taps, groups, False)
    lat_part = lat_pass(lon_part, lat_taps, groups, False)
    lifted = vertical_mix(vertical, lat_part)
    weighted = obs_weight * lifted
    back_vert = vertical_mix(vertical.T, weighted)
    back_lat = lat_pass(back_vert, lat_taps, groups, True)
    applied = direction + lon_pass(back_lat, lon_taps, groups, True)
    norm_old, curvature, crossed, squared = lax.psum(
        (
            jnp.sum(residual * residual),
            jnp.sum(direction * applied),
            jnp.sum(residual * applied),
            jnp.sum(applied * applied),
        ),
        ("lon", "lat"),
    )
    step_length = norm_old / curvature
    residual_next = residual - step_length * applied
    norm_new = norm_old - 2.0 * step_length * crossed + step_length * step_length * squared
    iterate_next = iterate + step_length * direction
    direction_next = residual_next + norm_new / norm_old * direction
    return (iterate_next, residual_next, direction_next)


def solution(mesh):
    placed = (
        P(None, "lat", "lon"),
        P(None, "lat", "lon"),
        P(None, "lat", "lon"),
        P(None, "lat", "lon"),
        P(),
        P(),
        P(),
        P(),
    )
    return jax.shard_map(
        local,
        mesh=mesh,
        in_specs=placed,
        out_specs=(P(None, "lat", "lon"), P(None, "lat", "lon"), P(None, "lat", "lon")),
        check_vma=False,
    )
```

profile of v0, /device:TPU:0, one launch (start us, length us, event | category | flops | bytes accessed | tf_op | source)
XLA Modules:
  0.0 138.4 jit_solution(3764943055885515981)
XLA Ops:
  0.7 0.9 constant_dynamic-update-slice_fusion.1
  1.6 0.5 collective-permute-start
  2.1 4.1 %collective-permute-start.1 = (f32[127,1,50]{2,0,1:T(8,128)S(1)}, f32[127,1,50]{2,0,1:T(8,128)S(1)}, u32[]{:S(2)}, u32[]{:S(2)}) collective-permute-start(f32[127,1,50]{2,0,1:T(8,128)S(1)} %get-tuple-element.20), channel_id=1, source_target_pairs={{4,0},{8,4},{12,8},{16,12},{20,16},{24,20},{28,24},{0,28},{5,1},{9... | collective-permute-start | bytes 76208 | tf_op jit(solution)/shard_map/ppermute | solution.py:24
  6.5 0.7 copy.65
  7.6 1.0 convolution_bitcast_fusion.3
  8.8 1.0 fusion.323
  19.6 9.6 %fusion.2 = f32[127,1,128]{2,1,0:T(1,128)S(1)} fusion(f32[127,101,1]{1,2,0:T(1,128)S(1)} %copy.85, f32[127,101,128]{2,0,1:T(8,128)S(1)} %bitcast.896), kind=kOutput, calls=%fused_computation.8 | convolution fusion | flops 19702272 | bytes 6683756 | tf_op jit(solution)/shard_map/lakb,lk->lab/dot_general | solution.py:76
  29.2 0.6 gather_fusion.2
  29.9 0.7 bitcast_select_fusion.4
  30.6 4.2 %all-to-all-start = ((f32[128,1,128]{2,1,0:T(1,128)}), f32[128,1,128]{2,1,0:T(1,128)S(1)}, u32[]{:S(2)}, u32[]{:S(2)}) async-start(f32[128,1,128]{2,1,0:T(1,128)} %bitcast.110), calls=%async_computation | async-start | bytes 131072 | tf_op jit(solution)/shard_map/all_to_all | solution.py:90
  34.8 0.6 gather_fusion.1
  35.4 4.2 %all-to-all-done = f32[128,1,128]{2,1,0:T(1,128)S(1)} async-done(((f32[128,1,128]{2,1,0:T(1,128)}), f32[128,1,128]{2,1,0:T(1,128)S(1)}, u32[]{:S(2)}, u32[]{:S(2)}) %all-to-all-start) | async-done | bytes 65568 | tf_op jit(solution)/shard_map/all_to_all | solution.py:90
  39.6 0.4 fusion.305
  40.0 0.6 copy.76
  40.6 3.3 %all-to-all-start.1 = ((f32[32,4,128]{2,0,1:T(8,128)}), f32[32,4,128]{2,0,1:T(8,128)S(1)}, u32[]{:S(2)}, u32[]{:S(2)}) async-start(f32[32,4,128]{2,0,1:T(8,128)} %copy.76), calls=%async_computation.1 | async-start | bytes 131072 | tf_op jit(solution)/shard_map/all_to_all | solution.py:93
  44.1 4.6 %all-to-all-done.1 = f32[32,4,128]{2,0,1:T(8,128)S(1)} async-done(((f32[32,4,128]{2,0,1:T(8,128)}), f32[32,4,128]{2,0,1:T(8,128)S(1)}, u32[]{:S(2)}, u32[]{:S(2)}) %all-to-all-start.1) | async-done | bytes 65568 | tf_op jit(solution)/shard_map/all_to_all | solution.py:93
  48.7 0.6 gather_fusion.3
  50.0 0.6 gather_fusion.4
  50.7 0.7 bitcast_select_fusion.1
  51.4 3.3 %all-to-all-start.2 = ((f32[128,1,128]{2,1,0:T(1,128)}), f32[128,1,128]{2,1,0:T(1,128)S(1)}, u32[]{:S(2)}, u32[]{:S(2)}) async-start(f32[128,1,128]{2,1,0:T(1,128)} %bitcast.127), calls=%async_computation.2 | async-start | bytes 131072 | tf_op jit(solution)/shard_map/all_to_all | solution.py:90
  54.9 0.6 gather_fusion
  55.6 3.9 %all-to-all-done.2 = f32[128,1,128]{2,1,0:T(1,128)S(1)} async-done(((f32[128,1,128]{2,1,0:T(1,128)}), f32[128,1,128]{2,1,0:T(1,128)S(1)}, u32[]{:S(2)}, u32[]{:S(2)}) %all-to-all-start.2) | async-done | bytes 65568 | tf_op jit(solution)/shard_map/all_to_all | solution.py:90
  59.9 0.6 copy.81
  60.5 3.3 %all-to-all-start.3 = ((f32[32,4,128]{2,0,1:T(8,128)}), f32[32,4,128]{2,0,1:T(8,128)S(1)}, u32[]{:S(2)}, u32[]{:S(2)}) async-start(f32[32,4,128]{2,0,1:T(8,128)} %copy.81), calls=%async_computation.3 | async-start | bytes 131072 | tf_op jit(solution)/shard_map/all_to_all | solution.py:93
  63.9 4.7 %all-to-all-done.3 = f32[32,4,128]{2,0,1:T(8,128)S(1)} async-done(((f32[32,4,128]{2,0,1:T(8,128)}), f32[32,4,128]{2,0,1:T(8,128)S(1)}, u32[]{:S(2)}, u32[]{:S(2)}) %all-to-all-start.3) | async-done | bytes 65568 | tf_op jit(solution)/shard_map/all_to_all | solution.py:93
  68.6 0.6 gather_fusion.5
  69.8 3.6 %collective-permute-start.3 = (f32[127,1,50]{2,0,1:T(8,128)S(1)}, f32[127,1,50]{2,0,1:T(8,128)S(1)}, u32[]{:S(2)}, u32[]{:S(2)}) collective-permute-start(f32[127,1,50]{2,0,1:T(8,128)S(1)} %get-tuple-element.18), channel_id=1, source_target_pairs={{4,0},{8,4},{12,8},{16,12},{20,16},{24,20},{28,24},{0,28},{5,1},{9... | collective-permute-start | bytes 76208 | tf_op jit(solution)/shard_map/ppermute | solution.py:24
  73.4 1.6 %collective-permute-done.2 = f32[127,1,50]{2,0,1:T(8,128)S(1)} collective-permute-done((f32[127,1,50]{2,0,1:T(8,128)S(1)}, f32[127,1,50]{2,0,1:T(8,128)S(1)}, u32[]{:S(2)}, u32[]{:S(2)}) %collective-permute-start.2) | collective-permute-done | bytes 25432 | tf_op jit(solution)/shard_map/ppermute | solution.py:22
  85.7 9.7 %fusion = f32[127,1,128]{2,1,0:T(1,128)S(1)} fusion(f32[127,101,1]{1,2,0:T(1,128)S(1)} %copy.88, f32[127,101,128]{2,0,1:T(8,128)S(1)} %bitcast.897), kind=kOutput, calls=%fused_computation.6 | convolution fusion | flops 19702272 | bytes 6683756 | tf_op jit(solution)/shard_map/lakb,lk->lab/dot_general | solution.py:76
  95.4 1.0 multiply_reduce_fusion
  96.4 37.3 %all-reduce.2 = (f32[]{:T(128)}, f32[]{:T(128)}, f32[]{:T(128)}, f32[]{:T(128)}) all-reduce(f32[]{:T(128)} %get-tuple-element.7, f32[]{:T(128)} %get-tuple-element.8, f32[]{:T(128)} %get-tuple-element.6, f32[]{:T(128)} %get-tuple-element.5), channel_id=1, replica_groups=mesh['lon'=8,'lat'=4] {'lon','lat'}, use_global_device_ids=true, to_apply=%region_1.2 | all-reduce | flops 4 | bytes 32 | tf_op jit(solution)/shard_map/psum | solution.py:112
  137.5 0.8 multiply_add_fusion
  (256 shorter events, 22.4 us)
Async XLA Ops:
  0.6 48.7 %copy-start = (f32[127,127]{1,0:T(8,128)S(1)}, f32[127,127]{1,0:T(8,128)}, u32[]{:S(2)}) copy-start(f32[127,127]{1,0:T(8,128)} %param.16) | copy-start | bytes 193552
  0.6 14.6 %copy-start.1 = (f32[127,1,128]{2,1,0:T(1,128)S(1)}, f32[127,1,128]{2,1,0:T(1,128)}, u32[]{:S(2)}) copy-start(f32[127,1,128]{2,1,0:T(1,128)} %param.14) | copy-start | bytes 195076
  1.6 8.3 %collective-permute-start = (f32[127,1,50]{2,0,1:T(8,128)S(1)}, f32[127,1,50]{2,0,1:T(8,128)S(1)}, u32[]{:S(2)}, u32[]{:S(2)}) collective-permute-start(f32[127,1,50]{2,0,1:T(8,128)S(1)} %get-tuple-element.21), channel_id=1, source_target_pairs={{0,4},{4,8},{8,12},{12,16},{16,20},{20,24},{24,28},{28,0},{1,5},{5... | collective-permute-start | bytes 76208 | tf_op jit(solution)/shard_map/ppermute | solution.py:22
  2.1 13.1 %collective-permute-start.1 = (f32[127,1,50]{2,0,1:T(8,128)S(1)}, f32[127,1,50]{2,0,1:T(8,128)S(1)}, u32[]{:S(2)}, u32[]{:S(2)}) collective-permute-start(f32[127,1,50]{2,0,1:T(8,128)S(1)} %get-tuple-element.20), channel_id=1, source_target_pairs={{4,0},{8,4},{12,8},{16,12},{20,16},{24,20},{28,24},{0,28},{5,1},{9... | collective-permute-start | bytes 76208 | tf_op jit(solution)/shard_map/ppermute | solution.py:24
  16.9 27.0 %copy-start.3 = (f32[32,101]{1,0:T(8,128)S(1)}, f32[32,101]{1,0:T(8,128)}, u32[]{:S(2)}) copy-start(f32[32,101]{1,0:T(8,128)} %param.18) | copy-start | bytes 38788
  16.9 27.1 %copy-start.5 = (f32[127,1,128]{2,1,0:T(1,128)S(1)}, f32[127,1,128]{2,1,0:T(1,128)}, u32[]{:S(2)}) copy-start(f32[127,1,128]{2,1,0:T(1,128)} %param.15) | copy-start | bytes 195076
  19.2 44.5 %copy-start.4 = (f32[32,101]{1,0:T(8,128)S(1)}, f32[32,101]{1,0:T(8,128)}, u32[]{:S(2)}) copy-start(f32[32,101]{1,0:T(8,128)} %param.17) | copy-start | bytes 38788
  30.6 9.0 %all-to-all-start = ((f32[128,1,128]{2,1,0:T(1,128)}), f32[128,1,128]{2,1,0:T(1,128)S(1)}, u32[]{:S(2)}, u32[]{:S(2)}) async-start(f32[128,1,128]{2,1,0:T(1,128)} %bitcast.110), calls=%async_computation | async-start | bytes 131072 | tf_op jit(solution)/shard_map/all_to_all | solution.py:90
  40.6 8.1 %all-to-all-start.1 = ((f32[32,4,128]{2,0,1:T(8,128)}), f32[32,4,128]{2,0,1:T(8,128)S(1)}, u32[]{:S(2)}, u32[]{:S(2)}) async-start(f32[32,4,128]{2,0,1:T(8,128)} %copy.76), calls=%async_computation.1 | async-start | bytes 131072 | tf_op jit(solution)/shard_map/all_to_all | solution.py:93
  51.4 8.1 %all-to-all-start.2 = ((f32[128,1,128]{2,1,0:T(1,128)}), f32[128,1,128]{2,1,0:T(1,128)S(1)}, u32[]{:S(2)}, u32[]{:S(2)}) async-start(f32[128,1,128]{2,1,0:T(1,128)} %bitcast.127), calls=%async_computation.2 | async-start | bytes 131072 | tf_op jit(solution)/shard_map/all_to_all | solution.py:90
  60.5 8.1 %all-to-all-start.3 = ((f32[32,4,128]{2,0,1:T(8,128)}), f32[32,4,128]{2,0,1:T(8,128)S(1)}, u32[]{:S(2)}, u32[]{:S(2)}) async-start(f32[32,4,128]{2,0,1:T(8,128)} %copy.81), calls=%async_computation.3 | async-start | bytes 131072 | tf_op jit(solution)/shard_map/all_to_all | solution.py:93
  69.4 5.6 %collective-permute-start.2 = (f32[127,1,50]{2,0,1:T(8,128)S(1)}, f32[127,1,50]{2,0,1:T(8,128)S(1)}, u32[]{:S(2)}, u32[]{:S(2)}) collective-permute-start(f32[127,1,50]{2,0,1:T(8,128)S(1)} %get-tuple-element.19), channel_id=1, source_target_pairs={{0,4},{4,8},{8,12},{12,16},{16,20},{20,24},{24,28},{28,0},{1,5},{5... | collective-permute-start | bytes 76208 | tf_op jit(solution)/shard_map/ppermute | solution.py:22
  69.8 10.6 %collective-permute-start.3 = (f32[127,1,50]{2,0,1:T(8,128)S(1)}, f32[127,1,50]{2,0,1:T(8,128)S(1)}, u32[]{:S(2)}, u32[]{:S(2)}) collective-permute-start(f32[127,1,50]{2,0,1:T(8,128)S(1)} %get-tuple-element.18), channel_id=1, source_target_pairs={{4,0},{8,4},{12,8},{16,12},{20,16},{24,20},{28,24},{0,28},{5,1},{9... | collective-permute-start | bytes 76208 | tf_op jit(solution)/shard_map/ppermute | solution.py:24
  82.3 13.1 %copy-start.2 = (f32[127,1,128]{2,1,0:T(1,128)S(1)}, f32[127,1,128]{2,1,0:T(1,128)}, u32[]{:S(2)}) copy-start(f32[127,1,128]{2,1,0:T(1,128)} %param.13) | copy-start | bytes 195076
  82.5 55.0 %copy-start.6 = (f32[127,1,128]{2,1,0:T(1,128)S(1)}, f32[127,1,128]{2,1,0:T(1,128)}, u32[]{:S(2)}) copy-start(f32[127,1,128]{2,1,0:T(1,128)} %param.12) | copy-start | bytes 195076
where the time goes:
time: 140 us; the launch traced here: 138 us
  blocking collectives  37.3 us (27%)
  matrix products  23.1 us (16%)
  starting transfers between devices  22.2 us (16%)
  waiting for transfers between devices  19 us (14%)
  other arithmetic  18.7 us (13%)
  local copies, waits for them, and re-layouts  12.1 us (9%)
  between operations  6.06 us (4%)
    psum x1, blocking collectives, local(): lax.psum((jnp.sum(residual * residual), jnp.sum(direction * applied), jnp...  37.3 us
    dot_general x2, matrix products, lon_pass(): return jnp.einsum('lakb,lk->lab', windows, kernels, precision=HIGHEST)  19.3 us
    unnamed x150, other arithmetic  14.6 us
    all_to_all x2, waiting for transfers between devices, lat_pass(): lax.all_to_all(filtered, 'lat', split_axis=1, concat_axis=0, tiled=True)  9.34 us
    all_to_all x2, waiting for transfers between devices, lat_pass(): lax.all_to_all(slotted, 'lat', split_axis=0, concat_axis=1, tiled=True)  8.02 us
    ppermute x2, starting transfers between devices, with_halo(): lax.ppermute(head, axis, [((i + 1) % count, i) for i in range(count)])  7.68 us
    all_to_all x2, starting transfers between devices, lat_pass(): lax.all_to_all(slotted, 'lat', split_axis=0, concat_axis=1, tiled=True)  7.43 us
    all_to_all x2, starting transfers between devices, lat_pass(): lax.all_to_all(filtered, 'lat', split_axis=1, concat_axis=0, tiled=True)  6.56 us
  transfers between devices with their start and end apart: 8, of which 5 were waited for; matrix products, arithmetic and copies ran while one was open for 11% of the time, Pallas kernels for 0%

commit v1 on v0

v1 whole, which is shorter than its diff:
```python
import functools

import jax
import jax.numpy as jnp
from jax import lax
from jax.experimental import pallas as pl
from jax.experimental.pallas import tpu as pltpu
from jax.sharding import PartitionSpec as P

LEV = 127
PADDED = 128
TAPS = 101
HALF = 50
GROUPS = 32
LANES = 128
SIDE = LANES // 2
FIRST = SIDE - HALF
STRIDE = 8
HIGHEST = lax.Precision.HIGHEST
MESH = pl.DeviceIdType.MESH
OWN, LEFT, RIGHT = 0, 1, 2


def shifted(low, high, lane, amount):
    if amount == 0:
        return low
    return jnp.where(
        lane < LANES - amount,
        pltpu.roll(low, LANES - amount, 1),
        pltpu.roll(high, LANES - amount, 1),
    )


def kernel(
    n_lon,
    n_lat,
    iterate_ref,
    residual_ref,
    direction_ref,
    weight_ref,
    vertical_ref,
    lon_taps_ref,
    lat_taps_ref,
    sizes_ref,
    iterate_out,
    residual_out,
    direction_out,
    held_d,
    held_r,
    held_b,
    matrix,
    flipped,
    gathered,
    gathered_r,
    window,
    lon_coef,
    lat_coef,
    filtered,
    image_part,
    lat_part,
    image,
    sums,
    sums_lat,
    sums_row,
    sums_lon,
    send_sem,
    recv_sem,
    back_send,
    back_recv,
    lat_send,
    lat_recv,
    lon_send,
    lon_recv,
):
    chunk = PADDED // n_lat
    tiles = chunk // 8
    my_lon, my_lat = lax.axis_index("lon"), lax.axis_index("lat")
    left = lax.rem(my_lon + n_lon - 1, n_lon)
    right = lax.rem(my_lon + 1, n_lon)

    def lat_at(step):
        return lax.rem(my_lat + step, n_lat)

    def rows_of(index):
        return pl.ds(pl.multiple_of(index * chunk, chunk), chunk)

    barrier = pltpu.get_barrier_semaphore()
    greeted = 0
    for step in range(n_lat):
        for lon in (my_lon, left, right):
            if step == 0 and lon is my_lon:
                continue
            pl.semaphore_signal(
                barrier, inc=1, device_id=(lon, lat_at(step)), device_id_type=MESH
            )
            greeted += 1
    for step in range(2, n_lon - 1):
        pl.semaphore_signal(
            barrier,
            inc=1,
            device_id=(lax.rem(my_lon + step, n_lon), my_lat),
            device_id_type=MESH,
        )
        greeted += 1

    held_d[pl.ds(PADDED - 8, 8), :] = jnp.zeros((8, LANES), jnp.float32)
    held_r[pl.ds(PADDED - 8, 8), :] = jnp.zeros((8, LANES), jnp.float32)
    held_d[pl.ds(0, LEV), :] = direction_ref[...]
    held_r[pl.ds(0, LEV), :] = residual_ref[...]

    pl.semaphore_wait(barrier, greeted)

    def send_block(held, phase, kind, step):
        to = lat_at(step)
        lon = (my_lon, left, right)[kind]
        slot = (OWN, RIGHT, LEFT)[kind]
        copy = pltpu.make_async_remote_copy(
            src_ref=held.at[rows_of(to), :],
            dst_ref=gathered.at[phase, slot, my_lat],
            send_sem=send_sem.at[phase, slot, to],
            recv_sem=recv_sem.at[phase, slot, my_lat],
            device_id=(lon, to),
            device_id_type=MESH,
        )
        copy.start()
        return copy

    def send_residual(step):
        to = lat_at(step)
        copy = pltpu.make_async_remote_copy(
            src_ref=held_r.at[rows_of(to), :],
            dst_ref=gathered_r.at[my_lat],
            send_sem=send_sem.at[0, 3, to],
            recv_sem=recv_sem.at[0, 3, my_lat],
            device_id=(my_lon, to),
            device_id_type=MESH,
        )
        copy.start()
        return copy

    def arrived(phase, kind, step):
        source = lat_at(step)
        place = gathered_r.at[source] if kind == 3 else gathered.at[phase, kind, source]
        pltpu.make_async_remote_copy(
            src_ref=place,
            dst_ref=place,
            send_sem=send_sem.at[phase, kind, source],
            recv_sem=recv_sem.at[phase, kind, source],
            device_id=(my_lon, source),
            device_id_type=MESH,
        ).wait_recv()

    def send_all(held, phase):
        copies = []
        for step in list(range(1, n_lat)) + [0]:
            for kind in (LEFT, RIGHT, OWN):
                if step or kind:
                    copies.append(send_block(held, phase, kind, step))
        gathered[phase, OWN, my_lat] = held[rows_of(my_lat), :]
        return copies

    def await_all(phase):
        for step in range(n_lat):
            for kind in (OWN, LEFT, RIGHT):
                if step or kind:
                    arrived(phase, kind, step)

    def send_back(parts, whole, phase):
        copies = []
        for step in range(1, n_lat):
            to = lat_at(step)
            copy = pltpu.make_async_remote_copy(
                src_ref=parts.at[to],
                dst_ref=whole.at[rows_of(my_lat), :],
                send_sem=back_send.at[phase, to],
                recv_sem=back_recv.at[phase, my_lat],
                device_id=(my_lon, to),
                device_id_type=MESH,
            )
            copy.start()
            copies.append(copy)
        whole[rows_of(my_lat), :] = parts[my_lat]
        return copies

    def await_back(whole, phase):
        for step in range(1, n_lat):
            source = lat_at(step)
            place = whole.at[rows_of(source), :]
            pltpu.make_async_remote_copy(
                src_ref=place,
                dst_ref=place,
                send_sem=back_send.at[phase, source],
                recv_sem=back_recv.at[phase, source],
                device_id=(my_lon, source),
                device_id_type=MESH,
            ).wait_recv()

    pending = send_all(held_d, 0)
    pending += [send_residual(step) for step in range(1, n_lat)]
    gathered_r[my_lat] = held_r[rows_of(my_lat), :]

    upto = (
        lax.broadcasted_iota(jnp.int32, (GROUPS, GROUPS), 0)
        <= lax.broadcasted_iota(jnp.int32, (GROUPS, GROUPS), 1)
    ).astype(jnp.float32)
    sizes = jnp.broadcast_to(sizes_ref[...].astype(jnp.float32), (8, GROUPS))
    bounds = jnp.dot(sizes, upto, precision=HIGHEST)[0:1, :]
    starts = bounds - sizes[0:1, :]
    level = (
        lax.broadcasted_iota(jnp.int32, (chunk, GROUPS), 0) + my_lat * chunk
    ).astype(jnp.float32)
    member = ((level > starts - 0.5) & (level < bounds - 0.5)).astype(jnp.float32)
    lon_rows = jnp.dot(member, lon_taps_ref[...], precision=HIGHEST)
    lat_rows = jnp.dot(member, lat_taps_ref[...], precision=HIGHEST)
    for tap in range(TAPS):
        lon_coef[tap] = jnp.broadcast_to(lon_rows[:, tap : tap + 1], (chunk, LANES))
    for offset in range(2 * n_lat - 1):
        tap = HALF - (n_lat - 1) + offset
        if 0 <= tap < TAPS:
            lat_coef[offset] = jnp.broadcast_to(lat_rows[:, tap : tap + 1], (chunk, LANES))
        else:
            lat_coef[offset] = jnp.zeros((chunk, LANES), jnp.float32)

    matrix[...] = jnp.zeros_like(matrix)
    matrix[pl.ds(0, LEV), pl.ds(0, LEV)] = vertical_ref[...]
    flipped[...] = matrix[...].T

    lane = lax.broadcasted_iota(jnp.int32, (8, LANES), 1)

    def filter_chunk(phase, adjoint, finish):
        def widen(at, _):
            row = pl.ds(pl.multiple_of(at * 8, 8), 8)
            for lat in range(n_lat):
                mine = pltpu.roll(gathered[phase, OWN, lat, row, :], SIDE, 1)
                before = pltpu.roll(gathered[phase, LEFT, lat, row, :], SIDE, 1)
                after = pltpu.roll(gathered[phase, RIGHT, lat, row, :], SIDE, 1)
                window[lat, 0, row, :] = jnp.where(lane < SIDE, before, mine)
                window[lat, 1, row, :] = jnp.where(lane < SIDE, mine, after)
            return 0

        lax.fori_loop(0, tiles, widen, 0)

        def one(at, _):
            out_lat = at // tiles
            row = pl.ds(pl.multiple_of(lax.rem(at, tiles) * 8, 8), 8)
            low = jnp.zeros((8, LANES), jnp.float32)
            high = jnp.zeros((8, LANES), jnp.float32)
            for lat in range(n_lat):
                offset = out_lat - lat if adjoint else lat - out_lat
                scale = lat_coef[offset + n_lat - 1, row, :]
                low = low + scale * window[lat, 0, row, :]
                high = high + scale * window[lat, 1, row, :]
            lows = [shifted(low, high, lane, j) for j in range(STRIDE)]
            highs = [shifted(high, low, lane, j) for j in range(STRIDE)]
            total = jnp.zeros((8, LANES), jnp.float32)
            for base in range(0, TAPS, STRIDE):
                part_low = part_high = None
                for j in range(min(STRIDE, TAPS - base)):
                    tap = base + j
                    scale = lon_coef[TAPS - 1 - tap if adjoint else tap, row, :]
                    if part_low is None:
                        part_low, part_high = scale * lows[j], scale * highs[j]
                    else:
                        part_low = part_low + scale * lows[j]
                        part_high = part_high + scale * highs[j]
                total = total + shifted(part_low, part_high, lane, FIRST + base)
            finish(out_lat, row, total)
            return 0

        lax.fori_loop(0, n_lat * tiles, one, 0)

    await_all(0)

    def keep(out_lat, row, total):
        filtered[out_lat, row, :] = total

    filter_chunk(0, False, keep)
    pending += send_back(filtered, lat_part, 0)
    await_back(lat_part, 0)

    lifted = jnp.dot(matrix[...], lat_part[...], precision=HIGHEST)
    held_b[...] = lifted
    held_b[pl.ds(0, LEV), :] = held_b[pl.ds(0, LEV), :] * weight_ref[...]
    held_b[...] = jnp.dot(flipped[...], held_b[...], precision=HIGHEST)

    pending += send_all(held_b, 1)
    for step in range(1, n_lat):
        arrived(0, 3, step)
    await_all(1)

    sums[...] = jnp.zeros_like(sums)

    def add(out_lat, row, total):
        total = total + gathered[0, OWN, out_lat, row, :]
        image_part[out_lat, row, :] = total
        old = gathered_r[out_lat, row, :]
        sums[0] += old * old
        sums[1] += total * gathered[0, OWN, out_lat, row, :]
        sums[2] += total * old
        sums[3] += total * total

    filter_chunk(1, True, add)
    pending += send_back(image_part, image, 1)

    def exchange(slots, send, recv, mine, count, to_device):
        copies = []
        for step in range(1, count):
            to = lax.rem(mine + step, count)
            copy = pltpu.make_async_remote_copy(
                src_ref=slots.at[mine],
                dst_ref=slots.at[mine],
                send_sem=send.at[to],
                recv_sem=recv.at[mine],
                device_id=to_device(to),
                device_id_type=MESH,
            )
            copy.start()
            copies.append(copy)
        for step in range(1, count):
            source = lax.rem(mine + step, count)
            pltpu.make_async_remote_copy(
                src_ref=slots.at[source],
                dst_ref=slots.at[source],
                send_sem=send.at[source],
                recv_sem=recv.at[source],
                device_id=to_device(source),
                device_id_type=MESH,
            ).wait_recv()
        total = slots[0]
        for index in range(1, count):
            total = total + slots[index]
        return total, copies

    rows = [jnp.sum(sums[i], axis=0, keepdims=True) for i in range(4)]
    sums_lat[my_lat] = jnp.concatenate(rows + [jnp.zeros((4, LANES), jnp.float32)], axis=0)
    total, copies = exchange(
        sums_lat, lat_send, lat_recv, my_lat, n_lat, lambda to: (my_lon, to)
    )
    pending += copies
    sums_lon[my_lon] = total
    total, copies = exchange(
        sums_lon, lon_send, lon_recv, my_lon, n_lon, lambda to: (to, my_lat)
    )
    pending += copies
    await_back(image, 1)

    total = jnp.sum(total, axis=1, keepdims=True)
    norm_old, curvature = total[0:1, :], total[1:2, :]
    crossed, squared = total[2:3, :], total[3:4, :]
    alpha = norm_old / curvature
    norm_new = norm_old - 2.0 * alpha * crossed + alpha * alpha * squared
    ratio = norm_new / norm_old
    direction = direction_ref[...]
    residual_next = residual_ref[...] - alpha * image[pl.ds(0, LEV), :]
    iterate_out[...] = iterate_ref[...] + alpha * direction
    residual_out[...] = residual_next
    direction_out[...] = residual_next + ratio * direction

    for copy in pending:
        copy.wait_send()


def local(n_lon, n_lat, iterate, residual, direction, obs_weight, vertical, lon_taps, lat_taps, band_sizes):
    chunk = PADDED // n_lat
    flat = [x.reshape(LEV, LANES) for x in (iterate, residual, direction, obs_weight)]
    f32 = jnp.float32
    vmem = pl.BlockSpec(memory_space=pltpu.VMEM)
    outs = pl.pallas_call(
        functools.partial(kernel, n_lon, n_lat),
        out_shape=[jax.ShapeDtypeStruct((LEV, LANES), f32)] * 3,
        in_specs=[vmem] * 8,
        out_specs=[vmem] * 3,
        scratch_shapes=[
            pltpu.VMEM((PADDED, LANES), f32),
            pltpu.VMEM((PADDED, LANES), f32),
            pltpu.VMEM((PADDED, LANES), f32),
            pltpu.VMEM((PADDED, PADDED), f32),
            pltpu.VMEM((PADDED, PADDED), f32),
            pltpu.VMEM((2, 3, n_lat, chunk, LANES), f32),
            pltpu.VMEM((n_lat, chunk, LANES), f32),
            pltpu.VMEM((n_lat, 2, chunk, LANES), f32),
            pltpu.VMEM((TAPS, chunk, LANES), f32),
            pltpu.VMEM((2 * n_lat - 1, chunk, LANES), f32),
            pltpu.VMEM((n_lat, chunk, LANES), f32),
            pltpu.VMEM((n_lat, chunk, LANES), f32),
            pltpu.VMEM((PADDED, LANES), f32),
            pltpu.VMEM((PADDED, LANES), f32),
            pltpu.VMEM((4, 8, LANES), f32),
            pltpu.VMEM((n_lat, 8, LANES), f32),
            pltpu.VMEM((8, LANES), f32),
            pltpu.VMEM((n_lon, 8, LANES), f32),
            pltpu.SemaphoreType.DMA((2, 4, n_lat)),
            pltpu.SemaphoreType.DMA((2, 4, n_lat)),
            pltpu.SemaphoreType.DMA((2, n_lat)),
            pltpu.SemaphoreType.DMA((2, n_lat)),
            pltpu.SemaphoreType.DMA((n_lat,)),
            pltpu.SemaphoreType.DMA((n_lat,)),
            pltpu.SemaphoreType.DMA((n_lon,)),
            pltpu.SemaphoreType.DMA((n_lon,)),
        ],
        compiler_params=pltpu.CompilerParams(
            collective_id=0,
            has_side_effects=True,
            vmem_limit_bytes=32 * 1024 * 1024,
        ),
    )(*flat, vertical, lon_taps, lat_taps, band_sizes.reshape(1, GROUPS))
    return tuple(x.reshape(LEV, 1, LANES) for x in outs)


def solution(mesh):
    field = P(None, "lat", "lon")
    return jax.shard_map(
        functools.partial(local, mesh.shape["lon"], mesh.shape["lat"]),
        mesh=mesh,
        in_specs=(field,) * 4 + (P(),) * 4,
        out_specs=(field,) * 3,
        check_vma=False,
    )
```

time: 140 us -> 38.2 us (0.27); the launches traced: 138 us -> 38 us
  blocking collectives: 37.3 us -> 0 us
  Pallas kernels: 0 us -> 33.5 us
  matrix products: 23.1 us -> 0 us
  starting transfers between devices: 22.2 us -> 0 us
  waiting for transfers between devices: 19 us -> 0 us
  other arithmetic: 18.7 us -> 0 us
  local copies, waits for them, and re-layouts: 12.1 us -> 3.8 us
  between operations: 6.06 us -> 0.72 us
    psum x1 -> x0, blocking collectives: 37.3 us -> none  [local(): lax.psum((jnp.sum(residual * residual), jnp.sum(direction * applied), jnp...]
    pallas_call x0 -> x1, Pallas kernels: none -> 33.5 us  [local(): pl.pallas_call(functools.partial(kernel, n_lon, n_lat), out_shape=[jax.Sh...]
    dot_general x10 -> x0, matrix products: 23.1 us -> none  [the longest x2 19.3 us: lon_pass(): return jnp.einsum('lakb,lk->lab', windows, kernels, precision=HIGHEST)]
    all_to_all x4 -> x0, waiting for transfers between devices: 17.4 us -> none  [the longest x2 9.34 us: lat_pass(): lax.all_to_all(filtered, 'lat', split_axis=1, concat_axis=0, tiled=True)]
    unnamed x150 -> x0, other arithmetic: 14.6 us -> none
    all_to_all x4 -> x0, starting transfers between devices: 14 us -> none  [the longest x2 7.43 us: lat_pass(): lax.all_to_all(slotted, 'lat', split_axis=0, concat_axis=1, tiled=True)]
    ppermute x4 -> x0, starting transfers between devices: 8.19 us -> none  [the longest x2 7.68 us: with_halo(): lax.ppermute(head, axis, [((i + 1) % count, i) for i in range(count)])]
    gather x8 -> x0, local copies, waits for them, and re-layouts: 3.93 us -> none  [the longest x4 1.35 us: band_matrices(): picked = kernel[:, jnp.clip(offsets, 0, TAPS - 1)]]
  transfers between devices with their start and end apart: 8 -> 0, of which waited for: 5 -> 0; matrix products, arithmetic and copies ran while one was open for 11% -> 0% of each run, Pallas kernels for 0% -> 0%
where the time goes in v1:
time: 38.2 us; the launch traced here: 38 us
  Pallas kernels  33.5 us (88%)
  local copies, waits for them, and re-layouts  3.8 us (10%)
  between operations  0.72 us (2%)
    pallas_call x1, Pallas kernels, local(): pl.pallas_call(functools.partial(kernel, n_lon, n_lat), out_shape=[jax.Sh...  33.5 us
    unnamed x17, local copies, waits for them, and re-layouts  3.8 us

profile of v1, /device:TPU:0, one launch (start us, length us, event | category | flops | bytes accessed | tf_op | source)
XLA Modules:
  0.0 38.0 jit_solution(8612536472634567849)
XLA Ops:
  0.6 0.0 copy-start.4
  0.6 0.0 copy-start.5
  0.7 0.9 %copy_bitcast_fusion.2 = (f32[127,128]{1,0:T(8,128)S(1)}, f32[127,128]{1,0:T(8,128)S(1)}) fusion(f32[127,1,128]{2,1,0:T(1,128)} %param.9, f32[127,1,128]{2,1,0:T(1,128)} %param.8), kind=kLoop, calls=%fused_computation.2 | loop fusion | bytes 260096
  1.6 0.0 copy-done.4
  1.6 0.0 copy-done.5
  1.6 0.0 copy-start
  1.6 0.0 copy-start.1
  1.6 0.0 copy-start.2
  1.6 0.0 copy-start.3
  1.7 0.8 %copy-done = f32[127,127]{1,0:T(8,128)S(1)} copy-done((f32[127,127]{1,0:T(8,128)S(1)}, f32[127,127]{1,0:T(8,128)}, u32[]{:S(2)}) %copy-start) | copy-done | bytes 64540
  2.4 0.0 copy-done.1
  2.4 0.0 copy-done.2
  2.4 0.0 copy-done.3
  2.4 33.5 %shard_map.103 = (f32[127,128]{1,0:T(8,128)S(1)}, f32[127,128]{1,0:T(8,128)S(1)}, f32[127,128]{1,0:T(8,128)S(1)}) custom-call(f32[127,128]{1,0:T(8,128)S(1)} %get-tuple-element.15.iterate_ref, f32[127,128]{1,0:T(8,128)S(1)} %get-tuple-element.14.residual_ref, f32[127,128]{1,0:T(8,128)S(1)} %get-tuple-element.13.direction_ref, ...), custom_call_target="tpu_custom_call" | custom-call | tf_op jit(solution)/shard_map/pallas_call | solution.py:368
  35.9 0.7 %copy.11 = f32[127,1,128]{2,1,0:T(1,128)} copy(f32[127,1,128]{2,0,1:T(8,128)S(1)} %bitcast.14) | data formatting | bytes 130048
  36.6 0.7 %copy.12 = f32[127,1,128]{2,1,0:T(1,128)} copy(f32[127,1,128]{2,0,1:T(8,128)S(1)} %bitcast.13) | data formatting | bytes 130048
  37.3 0.7 %copy.13 = f32[127,1,128]{2,1,0:T(1,128)} copy(f32[127,1,128]{2,0,1:T(8,128)S(1)} %bitcast.12) | data formatting | bytes 130048
  (1 shorter events, 0.0 us)
Async XLA Ops:
  0.6 0.9 %copy-start.4 = (f32[127,1,128]{2,1,0:T(1,128)S(1)}, f32[127,1,128]{2,1,0:T(1,128)}, u32[]{:S(2)}) copy-start(f32[127,1,128]{2,1,0:T(1,128)} %param.11) | copy-start | bytes 195076
  0.6 0.9 %copy-start.5 = (f32[127,1,128]{2,1,0:T(1,128)S(1)}, f32[127,1,128]{2,1,0:T(1,128)}, u32[]{:S(2)}) copy-start(f32[127,1,128]{2,1,0:T(1,128)} %param.10) | copy-start | bytes 195076
  1.6 0.8 %copy-start = (f32[127,127]{1,0:T(8,128)S(1)}, f32[127,127]{1,0:T(8,128)}, u32[]{:S(2)}) copy-start(f32[127,127]{1,0:T(8,128)} %vertical_ref.1) | copy-start | bytes 193552
  1.6 0.8 %copy-start.1 = (f32[32,101]{1,0:T(8,128)S(1)}, f32[32,101]{1,0:T(8,128)}, u32[]{:S(2)}) copy-start(f32[32,101]{1,0:T(8,128)} %lon_taps_ref.1) | copy-start | bytes 38788
  1.6 0.8 %copy-start.2 = (f32[32,101]{1,0:T(8,128)S(1)}, f32[32,101]{1,0:T(8,128)}, u32[]{:S(2)}) copy-start(f32[32,101]{1,0:T(8,128)} %lat_taps_ref.1) | copy-start | bytes 38788
  1.6 0.8 %copy-start.3 = (s32[32]{0:T(128)S(1)}, s32[32]{0:T(128)}, u32[]{:S(2)}) copy-start(s32[32]{0:T(128)} %param.15) | copy-start | bytes 388

commit v2 on v1

--- a/solution.py
+++ b/solution.py
@@ -16,6 +16,7 @@
 SIDE = LANES // 2
 FIRST = SIDE - HALF
 STRIDE = 8
+TOGETHER = 4
 HIGHEST = lax.Precision.HIGHEST
 MESH = pl.DeviceIdType.MESH
 OWN, LEFT, RIGHT = 0, 1, 2
@@ -34,17 +35,26 @@
 def kernel(
     n_lon,
     n_lat,
-    iterate_ref,
-    residual_ref,
-    direction_ref,
-    weight_ref,
+    iterate_hbm,
+    residual_hbm,
+    direction_hbm,
+    weight_hbm,
+    vertical_hbm,
+    lon_taps_hbm,
+    lat_taps_hbm,
+    sizes_hbm,
+    iterate_out,
+    residual_out,
+    direction_out,
+    held_i,
+    held_w,
     vertical_ref,
     lon_taps_ref,
     lat_taps_ref,
     sizes_ref,
-    iterate_out,
-    residual_out,
-    direction_out,
+    nexts,
+    load_sem,
+    store_sem,
     held_d,
     held_r,
     held_b,
@@ -53,6 +63,7 @@
     gathered,
     gathered_r,
     window,
+    shifts,
     lon_coef,
     lat_coef,
     filtered,
@@ -61,8 +72,7 @@
     image,
     sums,
     sums_lat,
-    sums_row,
-    sums_lon,
+    sums_all,
     send_sem,
     recv_sem,
     back_send,
@@ -74,6 +84,7 @@
 ):
     chunk = PADDED // n_lat
     tiles = chunk // 8
+    direct = n_lon * n_lat <= 64
     my_lon, my_lat = lax.axis_index("lon"), lax.axis_index("lat")
     left = lax.rem(my_lon + n_lon - 1, n_lon)
     right = lax.rem(my_lon + 1, n_lon)
@@ -83,6 +94,23 @@
 
     def rows_of(index):
         return pl.ds(pl.multiple_of(index * chunk, chunk), chunk)
+
+    def load(source, place, index):
+        copy = pltpu.make_async_copy(source, place, load_sem.at[index])
+        copy.start()
+        return copy
+
+    levels = pl.ds(0, LEV)
+    loads = [
+        load(direction_hbm.at[:, 0, :], held_d.at[levels, :], 0),
+        load(residual_hbm.at[:, 0, :], held_r.at[levels, :], 1),
+        load(sizes_hbm, sizes_ref, 2),
+        load(lon_taps_hbm, lon_taps_ref, 3),
+        load(lat_taps_hbm, lat_taps_ref, 4),
+        load(vertical_hbm, vertical_ref, 5),
+        load(weight_hbm.at[:, 0, :], held_w.at[levels, :], 6),
+        load(iterate_hbm.at[:, 0, :], held_i.at[levels, :], 7),
+    ]
 
     barrier = pltpu.get_barrier_semaphore()
     greeted = 0
@@ -94,19 +122,20 @@
                 barrier, inc=1, device_id=(lon, lat_at(step)), device_id_type=MESH
             )
             greeted += 1
-    for step in range(2, n_lon - 1):
-        pl.semaphore_signal(
-            barrier,
-            inc=1,
-            device_id=(lax.rem(my_lon + step, n_lon), my_lat),
-            device_id_type=MESH,
-        )
-        greeted += 1
-
-    held_d[pl.ds(PADDED - 8, 8), :] = jnp.zeros((8, LANES), jnp.float32)
-    held_r[pl.ds(PADDED - 8, 8), :] = jnp.zeros((8, LANES), jnp.float32)
-    held_d[pl.ds(0, LEV), :] = direction_ref[...]
-    held_r[pl.ds(0, LEV), :] = residual_ref[...]
+    for across in range(n_lat if direct else 1):
+        for step in range(2, n_lon - 1):
+            pl.semaphore_signal(
+                barrier,
+                inc=1,
+                device_id=(lax.rem(my_lon + step, n_lon), lat_at(across)),
+                device_id_type=MESH,
+            )
+            greeted += 1
+
+    held_d[pl.ds(LEV, 1), :] = jnp.zeros((1, LANES), jnp.float32)
+    held_r[pl.ds(LEV, 1), :] = jnp.zeros((1, LANES), jnp.float32)
+    loads[0].wait()
+    loads[1].wait()
 
     pl.semaphore_wait(barrier, greeted)
 
@@ -198,6 +227,9 @@
     pending = send_all(held_d, 0)
     pending += [send_residual(step) for step in range(1, n_lat)]
     gathered_r[my_lat] = held_r[rows_of(my_lat), :]
+
+    for copy in loads[2:6]:
+        copy.wait()
 
     upto = (
         lax.broadcasted_iota(jnp.int32, (GROUPS, GROUPS), 0)
@@ -228,47 +260,50 @@
     lane = lax.broadcasted_iota(jnp.int32, (8, LANES), 1)
 
     def filter_chunk(phase, adjoint, finish):
-        def widen(at, _):
-            row = pl.ds(pl.multiple_of(at * 8, 8), 8)
+        for at in range(tiles):
+            row = pl.ds(at * 8, 8)
             for lat in range(n_lat):
                 mine = pltpu.roll(gathered[phase, OWN, lat, row, :], SIDE, 1)
                 before = pltpu.roll(gathered[phase, LEFT, lat, row, :], SIDE, 1)
                 after = pltpu.roll(gathered[phase, RIGHT, lat, row, :], SIDE, 1)
                 window[lat, 0, row, :] = jnp.where(lane < SIDE, before, mine)
                 window[lat, 1, row, :] = jnp.where(lane < SIDE, mine, after)
-            return 0
-
-        lax.fori_loop(0, tiles, widen, 0)
-
-        def one(at, _):
-            out_lat = at // tiles
-            row = pl.ds(pl.multiple_of(lax.rem(at, tiles) * 8, 8), 8)
-            low = jnp.zeros((8, LANES), jnp.float32)
-            high = jnp.zeros((8, LANES), jnp.float32)
-            for lat in range(n_lat):
-                offset = out_lat - lat if adjoint else lat - out_lat
-                scale = lat_coef[offset + n_lat - 1, row, :]
-                low = low + scale * window[lat, 0, row, :]
-                high = high + scale * window[lat, 1, row, :]
-            lows = [shifted(low, high, lane, j) for j in range(STRIDE)]
-            highs = [shifted(high, low, lane, j) for j in range(STRIDE)]
-            total = jnp.zeros((8, LANES), jnp.float32)
+
+        def some(at, _):
+            first = lax.rem(at, n_lat // TOGETHER) * TOGETHER
+            row = pl.ds(pl.multiple_of(at // (n_lat // TOGETHER) * 8, 8), 8)
+            for out in range(TOGETHER):
+                low = jnp.zeros((8, LANES), jnp.float32)
+                high = jnp.zeros((8, LANES), jnp.float32)
+                for lat in range(n_lat):
+                    offset = first + (out - lat) if adjoint else lat - out - first
+                    scale = lat_coef[offset + n_lat - 1, row, :]
+                    low = low + scale * window[lat, 0, row, :]
+                    high = high + scale * window[lat, 1, row, :]
+                for j in range(STRIDE):
+                    shifts[out, 0, j] = shifted(low, high, lane, j)
+                    shifts[out, 1, j] = shifted(high, low, lane, j)
+            totals = [jnp.zeros((8, LANES), jnp.float32)] * TOGETHER
             for base in range(0, TAPS, STRIDE):
-                part_low = part_high = None
+                parts = [None] * TOGETHER
                 for j in range(min(STRIDE, TAPS - base)):
                     tap = base + j
                     scale = lon_coef[TAPS - 1 - tap if adjoint else tap, row, :]
-                    if part_low is None:
-                        part_low, part_high = scale * lows[j], scale * highs[j]
-                    else:
-                        part_low = part_low + scale * lows[j]
-                        part_high = part_high + scale * highs[j]
-                total = total + shifted(part_low, part_high, lane, FIRST + base)
-            finish(out_lat, row, total)
+                    for out in range(TOGETHER):
+                        low, high = scale * shifts[out, 0, j], scale * shifts[out, 1, j]
+                        if parts[out] is not None:
+                            low, high = parts[out][0] + low, parts[out][1] + high
+                        parts[out] = low, high
+                for out in range(TOGETHER):
+                    totals[out] = totals[out] + shifted(*parts[out], lane, FIRST + base)
+            for out in range(TOGETHER):
+                finish(first + out, row, totals[out])
             return 0
 
-        lax.fori_loop(0, n_lat * tiles, one, 0)
-
+        lax.fori_loop(0, tiles * (n_lat // TOGETHER), some, 0)
+
+    loads[6].wait()
+    loads[7].wait()
     await_all(0)
 
     def keep(out_lat, row, total):
@@ -280,7 +315,7 @@
 
     lifted = jnp.dot(matrix[...], lat_part[...], precision=HIGHEST)
     held_b[...] = lifted
-    held_b[pl.ds(0, LEV), :] = held_b[pl.ds(0, LEV), :] * weight_ref[...]
+    held_b[pl.ds(0, LEV), :] = held_b[pl.ds(0, LEV), :] * held_w[levels, :]
     held_b[...] = jnp.dot(flipped[...], held_b[...], precision=HIGHEST)
 
     pending += send_all(held_b, 1)
@@ -332,16 +367,30 @@
         return total, copies
 
     rows = [jnp.sum(sums[i], axis=0, keepdims=True) for i in range(4)]
-    sums_lat[my_lat] = jnp.concatenate(rows + [jnp.zeros((4, LANES), jnp.float32)], axis=0)
-    total, copies = exchange(
-        sums_lat, lat_send, lat_recv, my_lat, n_lat, lambda to: (my_lon, to)
-    )
-    pending += copies
-    sums_lon[my_lon] = total
-    total, copies = exchange(
-        sums_lon, lon_send, lon_recv, my_lon, n_lon, lambda to: (to, my_lat)
-    )
-    pending += copies
+    mine = jnp.concatenate(rows + [jnp.zeros((4, LANES), jnp.float32)], axis=0)
+    if direct:
+        me = my_lon * n_lat + my_lat
+        sums_all[me] = mine
+        total, copies = exchange(
+            sums_all,
+            lon_send,
+            lon_recv,
+            me,
+            n_lon * n_lat,
+            lambda to: (to // n_lat, lax.rem(to, n_lat)),
+        )
+        pending += copies
+    else:
+        sums_lat[my_lat] = mine
+        total, copies = exchange(
+            sums_lat, lat_send, lat_recv, my_lat, n_lat, lambda to: (my_lon, to)
+        )
+        pending += copies
+        sums_all[my_lon] = total
+        total, copies = exchange(
+            sums_all, lon_send, lon_recv, my_lon, n_lon, lambda to: (to, my_lat)
+        )
+        pending += copies
     await_back(image, 1)
 
     total = jnp.sum(total, axis=1, keepdims=True)
@@ -350,27 +399,45 @@
     alpha = norm_old / curvature
     norm_new = norm_old - 2.0 * alpha * crossed + alpha * alpha * squared
     ratio = norm_new / norm_old
-    direction = direction_ref[...]
-    residual_next = residual_ref[...] - alpha * image[pl.ds(0, LEV), :]
-    iterate_out[...] = iterate_ref[...] + alpha * direction
-    residual_out[...] = residual_next
-    direction_out[...] = residual_next + ratio * direction
+    direction = held_d[levels, :]
+    residual_next = held_r[levels, :] - alpha * image[levels, :]
+    nexts[0, levels, :] = held_i[levels, :] + alpha * direction
+    nexts[1, levels, :] = residual_next
+    nexts[2, levels, :] = residual_next + ratio * direction
+    stores = []
+    for index, out in enumerate((iterate_out, residual_out, direction_out)):
+        copy = pltpu.make_async_copy(
+            nexts.at[index, levels, :], out.at[:, 0, :], store_sem.at[index]
+        )
+        copy.start()
+        stores.append(copy)
 
     for copy in pending:
         copy.wait_send()
+    for copy in stores:
+        copy.wait()
 
 
 def local(n_lon, n_lat, iterate, residual, direction, obs_weight, vertical, lon_taps, lat_taps, band_sizes):
     chunk = PADDED // n_lat
-    flat = [x.reshape(LEV, LANES) for x in (iterate, residual, direction, obs_weight)]
+    last = n_lon * n_lat if n_lon * n_lat <= 64 else n_lon
     f32 = jnp.float32
-    vmem = pl.BlockSpec(memory_space=pltpu.VMEM)
-    outs = pl.pallas_call(
+    hbm = pl.BlockSpec(memory_space=pltpu.HBM)
+    return pl.pallas_call(
         functools.partial(kernel, n_lon, n_lat),
-        out_shape=[jax.ShapeDtypeStruct((LEV, LANES), f32)] * 3,
-        in_specs=[vmem] * 8,
-        out_specs=[vmem] * 3,
+        out_shape=[jax.ShapeDtypeStruct((LEV, 1, LANES), f32)] * 3,
+        in_specs=[hbm] * 8,
+        out_specs=[hbm] * 3,
         scratch_shapes=[
+            pltpu.VMEM((PADDED, LANES), f32),
+            pltpu.VMEM((PADDED, LANES), f32),
+            pltpu.VMEM((LEV, LEV), f32),
+            pltpu.VMEM((GROUPS, TAPS), f32),
+            pltpu.VMEM((GROUPS, TAPS), f32),
+            pltpu.VMEM((1, GROUPS), jnp.int32),
+            pltpu.VMEM((3, PADDED, LANES), f32),
+            pltpu.SemaphoreType.DMA((8,)),
+            pltpu.SemaphoreType.DMA((3,)),
             pltpu.VMEM((PADDED, LANES), f32),
             pltpu.VMEM((PADDED, LANES), f32),
             pltpu.VMEM((PADDED, LANES), f32),
@@ -379,6 +446,7 @@
             pltpu.VMEM((2, 3, n_lat, chunk, LANES), f32),
             pltpu.VMEM((n_lat, chunk, LANES), f32),
             pltpu.VMEM((n_lat, 2, chunk, LANES), f32),
+            pltpu.VMEM((TOGETHER, 2, STRIDE, 8, LANES), f32),
             pltpu.VMEM((TAPS, chunk, LANES), f32),
             pltpu.VMEM((2 * n_lat - 1, chunk, LANES), f32),
             pltpu.VMEM((n_lat, chunk, LANES), f32),
@@ -387,24 +455,31 @@
             pltpu.VMEM((PADDED, LANES), f32),
             pltpu.VMEM((4, 8, LANES), f32),
             pltpu.VMEM((n_lat, 8, LANES), f32),
-            pltpu.VMEM((8, LANES), f32),
-            pltpu.VMEM((n_lon, 8, LANES), f32),
+            pltpu.VMEM((last, 8, LANES), f32),
             pltpu.SemaphoreType.DMA((2, 4, n_lat)),
             pltpu.SemaphoreType.DMA((2, 4, n_lat)),
             pltpu.SemaphoreType.DMA((2, n_lat)),
             pltpu.SemaphoreType.DMA((2, n_lat)),
             pltpu.SemaphoreType.DMA((n_lat,)),
             pltpu.SemaphoreType.DMA((n_lat,)),
-            pltpu.SemaphoreType.DMA((n_lon,)),
-            pltpu.SemaphoreType.DMA((n_lon,)),
+            pltpu.SemaphoreType.DMA((last,)),
+            pltpu.SemaphoreType.DMA((last,)),
         ],
         compiler_params=pltpu.CompilerParams(
             collective_id=0,
             has_side_effects=True,
-            vmem_limit_bytes=32 * 1024 * 1024,
+            vmem_limit_bytes=64 * 1024 * 1024,
         ),
-    )(*flat, vertical, lon_taps, lat_taps, band_sizes.reshape(1, GROUPS))
-    return tuple(x.reshape(LEV, 1, LANES) for x in outs)
+    )(
+        iterate,
+        residual,
+        direction,
+        obs_weight,
+        vertical,
+        lon_taps,
+        lat_taps,
+        band_sizes.reshape(1, GROUPS),
+    )
 
 
 def solution(mesh):

time: 38.2 us -> 33.5 us (0.88)
  Pallas kernels: 33.5 us -> 29.6 us
  local copies, waits for them, and re-layouts: 3.8 us -> 2.98 us
    pallas_call x1, Pallas kernels: 33.5 us -> 29.6 us  [local(): pl.pallas_call(functools.partial(kernel, n_lon, n_lat), out_shape=[jax.Sh...]
    unnamed x17 -> x7, local copies, waits for them, and re-layouts: 3.8 us -> 2.98 us
where the time goes in v2:
time: 33.5 us; the launch traced here: 33.2 us
  Pallas kernels  29.6 us (88%)
  local copies, waits for them, and re-layouts  2.98 us (9%)
  between operations  0.65 us (2%)
    pallas_call x1, Pallas kernels, local(): pl.pallas_call(functools.partial(kernel, n_lon, n_lat), out_shape=[jax.Sh...  29.6 us
    unnamed x7, local copies, waits for them, and re-layouts  2.98 us

profile of v2, /device:TPU:0, one launch (start us, length us, event | category | flops | bytes accessed | tf_op | source)
XLA Modules:
  0.0 33.2 jit_solution(11321215967272463821)
XLA Ops:
  0.6 29.6 %shard_map.103 = (f32[127,1,128]{2,1,0:T(1,128)}, f32[127,1,128]{2,1,0:T(1,128)}, f32[127,1,128]{2,1,0:T(1,128)}) custom-call(f32[127,1,128]{2,1,0:T(1,128)} %iterate_hbm.1, f32[127,1,128]{2,1,0:T(1,128)} %residual_hbm.1, f32[127,1,128]{2,1,0:T(1,128)} %direction_hbm.1, f32[127,1,128]{2,1,0:T(1,128)} %weight_hbm.1, f32[127,127]{1,0:T(8,128)} %vertical_hbm.1, ...), custom_call_target="tpu_custom_call" | custom-call | tf_op jit(solution)/shard_map/pallas_call | solution.py:426
  30.3 0.0 copy-start.1
  30.3 1.5 %copy.14 = f32[127,1,128]{2,1,0:T(1,128)} copy(f32[127,1,128]{2,1,0:T(1,128)} %get-tuple-element.6) | data formatting | bytes 130048
  31.8 0.0 copy-done.1
  31.8 0.0 copy-start
  31.8 0.6 %copy.15 = f32[127,1,128]{2,1,0:T(1,128)} copy(f32[127,1,128]{2,1,0:T(1,128)S(1)} %copy-done.1) | data formatting | bytes 130048
  32.4 0.2 copy-done
  32.6 0.6 %copy.16 = f32[127,1,128]{2,1,0:T(1,128)} copy(f32[127,1,128]{2,1,0:T(1,128)S(1)} %copy-done) | data formatting | bytes 130048
Async XLA Ops:
  30.3 1.5 %copy-start.1 = (f32[127,1,128]{2,1,0:T(1,128)S(1)}, f32[127,1,128]{2,1,0:T(1,128)}, u32[]{:S(2)}) copy-start(f32[127,1,128]{2,1,0:T(1,128)} %get-tuple-element.7) | copy-start | bytes 195076
  31.8 0.9 %copy-start = (f32[127,1,128]{2,1,0:T(1,128)S(1)}, f32[127,1,128]{2,1,0:T(1,128)}, u32[]{:S(2)}) copy-start(f32[127,1,128]{2,1,0:T(1,128)} %get-tuple-element.8) | copy-start | bytes 195076

commit v3 on v2

--- a/solution.py
+++ b/solution.py
@@ -35,7 +35,6 @@
 def kernel(
     n_lon,
     n_lat,
-    iterate_hbm,
     residual_hbm,
     direction_hbm,
     weight_hbm,
@@ -43,16 +42,15 @@
     lon_taps_hbm,
     lat_taps_hbm,
     sizes_hbm,
-    iterate_out,
-    residual_out,
-    direction_out,
-    held_i,
+    image_out,
+    alpha_out,
+    ratio_out,
     held_w,
     vertical_ref,
     lon_taps_ref,
     lat_taps_ref,
     sizes_ref,
-    nexts,
+    scales,
     load_sem,
     store_sem,
     held_d,
@@ -62,6 +60,8 @@
     flipped,
     gathered,
     gathered_r,
+    sides,
+    sides_in,
     window,
     shifts,
     lon_coef,
@@ -85,6 +85,8 @@
     chunk = PADDED // n_lat
     tiles = chunk // 8
     direct = n_lon * n_lat <= 64
+    packed = tiles % 2 == 0
+    lane = lax.broadcasted_iota(jnp.int32, (8, LANES), 1)
     my_lon, my_lat = lax.axis_index("lon"), lax.axis_index("lat")
     left = lax.rem(my_lon + n_lon - 1, n_lon)
     right = lax.rem(my_lon + 1, n_lon)
@@ -109,7 +111,6 @@
         load(lat_taps_hbm, lat_taps_ref, 4),
         load(vertical_hbm, vertical_ref, 5),
         load(weight_hbm.at[:, 0, :], held_w.at[levels, :], 6),
-        load(iterate_hbm.at[:, 0, :], held_i.at[levels, :], 7),
     ]
 
     barrier = pltpu.get_barrier_semaphore()
@@ -137,10 +138,10 @@
     loads[0].wait()
     loads[1].wait()
 
-    pl.semaphore_wait(barrier, greeted)
-
     def send_block(held, phase, kind, step):
         to = lat_at(step)
+        if packed and kind != OWN:
+            return send_side(phase, kind, to)
         lon = (my_lon, left, right)[kind]
         slot = (OWN, RIGHT, LEFT)[kind]
         copy = pltpu.make_async_remote_copy(
@@ -154,6 +155,29 @@
         copy.start()
         return copy
 
+    def send_side(phase, kind, to):
+        lon, slot = ((left, 1), (right, 0))[kind - LEFT]
+        copy = pltpu.make_async_remote_copy(
+            src_ref=sides.at[phase, slot, to],
+            dst_ref=sides_in.at[phase, slot, my_lat],
+            send_sem=send_sem.at[phase, 1 + slot, to],
+            recv_sem=recv_sem.at[phase, 1 + slot, my_lat],
+            device_id=(lon, to),
+            device_id_type=MESH,
+        )
+        copy.start()
+        return copy
+
+    def pack(held, phase):
+        for lat in range(n_lat):
+            for at in range(tiles // 2):
+                first = held[pl.ds(lat * chunk + at * 8, 8), :]
+                second = held[pl.ds(lat * chunk + chunk // 2 + at * 8, 8), :]
+                turned = pltpu.roll(first, SIDE, 1)
+                row = pl.ds(at * 8, 8)
+                sides[phase, 0, lat, row, :] = jnp.where(lane < SIDE, turned, second)
+                sides[phase, 1, lat, row, :] = jnp.where(lane < SIDE, second, turned)
+
     def send_residual(step):
         to = lat_at(step)
         copy = pltpu.make_async_remote_copy(
@@ -169,7 +193,12 @@
 
     def arrived(phase, kind, step):
         source = lat_at(step)
-        place = gathered_r.at[source] if kind == 3 else gathered.at[phase, kind, source]
+        if kind == 3:
+            place = gathered_r.at[source]
+        elif packed and kind != OWN:
+            place = sides_in.at[phase, kind - LEFT, source]
+        else:
+            place = gathered.at[phase, kind, source]
         pltpu.make_async_remote_copy(
             src_ref=place,
             dst_ref=place,
@@ -224,8 +253,10 @@
                 device_id_type=MESH,
             ).wait_recv()
 
+    if packed:
+        pack(held_d, 0)
+    pl.semaphore_wait(barrier, greeted)
     pending = send_all(held_d, 0)
-    pending += [send_residual(step) for step in range(1, n_lat)]
     gathered_r[my_lat] = held_r[rows_of(my_lat), :]
 
     for copy in loads[2:6]:
@@ -257,15 +288,22 @@
     matrix[pl.ds(0, LEV), pl.ds(0, LEV)] = vertical_ref[...]
     flipped[...] = matrix[...].T
 
-    lane = lax.broadcasted_iota(jnp.int32, (8, LANES), 1)
 
     def filter_chunk(phase, adjoint, finish):
         for at in range(tiles):
             row = pl.ds(at * 8, 8)
             for lat in range(n_lat):
                 mine = pltpu.roll(gathered[phase, OWN, lat, row, :], SIDE, 1)
-                before = pltpu.roll(gathered[phase, LEFT, lat, row, :], SIDE, 1)
-                after = pltpu.roll(gathered[phase, RIGHT, lat, row, :], SIDE, 1)
+                if packed:
+                    half = pl.ds(at % (tiles // 2) * 8, 8)
+                    before = sides_in[phase, 0, lat, half, :]
+                    after = sides_in[phase, 1, lat, half, :]
+                else:
+                    before = gathered[phase, LEFT, lat, row, :]
+                    after = gathered[phase, RIGHT, lat, row, :]
+                if not packed or at >= tiles // 2:
+                    before = pltpu.roll(before, SIDE, 1)
+                    after = pltpu.roll(after, SIDE, 1)
                 window[lat, 0, row, :] = jnp.where(lane < SIDE, before, mine)
                 window[lat, 1, row, :] = jnp.where(lane < SIDE, mine, after)
 
@@ -303,8 +341,9 @@
         lax.fori_loop(0, tiles * (n_lat // TOGETHER), some, 0)
 
     loads[6].wait()
-    loads[7].wait()
     await_all(0)
+
+    pending += [send_residual(step) for step in range(1, n_lat)]
 
     def keep(out_lat, row, total):
         filtered[out_lat, row, :] = total
@@ -318,6 +357,8 @@
     held_b[pl.ds(0, LEV), :] = held_b[pl.ds(0, LEV), :] * held_w[levels, :]
     held_b[...] = jnp.dot(flipped[...], held_b[...], precision=HIGHEST)
 
+    if packed:
+        pack(held_b, 1)
     pending += send_all(held_b, 1)
     for step in range(1, n_lat):
         arrived(0, 3, step)
@@ -337,7 +378,7 @@
     filter_chunk(1, True, add)
     pending += send_back(image_part, image, 1)
 
-    def exchange(slots, send, recv, mine, count, to_device):
+    def exchange(slots, send, recv, mine, count, to_device, between=lambda: None):
         copies = []
         for step in range(1, count):
             to = lax.rem(mine + step, count)
@@ -351,6 +392,7 @@
             )
             copy.start()
             copies.append(copy)
+        between()
         for step in range(1, count):
             source = lax.rem(mine + step, count)
             pltpu.make_async_remote_copy(
@@ -366,6 +408,14 @@
             total = total + slots[index]
         return total, copies
 
+    store = pltpu.make_async_copy(
+        image.at[levels, :], image_out.at[:, 0, :], store_sem.at[0]
+    )
+
+    def put_image():
+        await_back(image, 1)
+        store.start()
+
     rows = [jnp.sum(sums[i], axis=0, keepdims=True) for i in range(4)]
     mine = jnp.concatenate(rows + [jnp.zeros((4, LANES), jnp.float32)], axis=0)
     if direct:
@@ -378,6 +428,7 @@
             me,
             n_lon * n_lat,
             lambda to: (to // n_lat, lax.rem(to, n_lat)),
+            put_image,
         )
         pending += copies
     else:
@@ -388,26 +439,21 @@
         pending += copies
         sums_all[my_lon] = total
         total, copies = exchange(
-            sums_all, lon_send, lon_recv, my_lon, n_lon, lambda to: (to, my_lat)
+            sums_all, lon_send, lon_recv, my_lon, n_lon, lambda to: (to, my_lat), put_image
         )
         pending += copies
-    await_back(image, 1)
-
     total = jnp.sum(total, axis=1, keepdims=True)
     norm_old, curvature = total[0:1, :], total[1:2, :]
     crossed, squared = total[2:3, :], total[3:4, :]
     alpha = norm_old / curvature
     norm_new = norm_old - 2.0 * alpha * crossed + alpha * alpha * squared
     ratio = norm_new / norm_old
-    direction = held_d[levels, :]
-    residual_next = held_r[levels, :] - alpha * image[levels, :]
-    nexts[0, levels, :] = held_i[levels, :] + alpha * direction
-    nexts[1, levels, :] = residual_next
-    nexts[2, levels, :] = residual_next + ratio * direction
-    stores = []
-    for index, out in enumerate((iterate_out, residual_out, direction_out)):
+    scales[0] = jnp.broadcast_to(alpha, (1, LANES))
+    scales[1] = jnp.broadcast_to(ratio, (1, LANES))
+    stores = [store]
+    for index, out in enumerate((alpha_out, ratio_out)):
         copy = pltpu.make_async_copy(
-            nexts.at[index, levels, :], out.at[:, 0, :], store_sem.at[index]
+            scales.at[pl.ds(index, 1)], out, store_sem.at[1 + index]
         )
         copy.start()
         stores.append(copy)
@@ -422,21 +468,25 @@
     chunk = PADDED // n_lat
     last = n_lon * n_lat if n_lon * n_lat <= 64 else n_lon
     f32 = jnp.float32
+    side_shape = (2, 2, n_lat, max(8, chunk // 2), LANES)
     hbm = pl.BlockSpec(memory_space=pltpu.HBM)
-    return pl.pallas_call(
+    image, alpha, ratio = pl.pallas_call(
         functools.partial(kernel, n_lon, n_lat),
-        out_shape=[jax.ShapeDtypeStruct((LEV, 1, LANES), f32)] * 3,
-        in_specs=[hbm] * 8,
+        out_shape=[
+            jax.ShapeDtypeStruct((LEV, 1, LANES), f32),
+            jax.ShapeDtypeStruct((1, 1, LANES), f32),
+            jax.ShapeDtypeStruct((1, 1, LANES), f32),
+        ],
+        in_specs=[hbm] * 7,
         out_specs=[hbm] * 3,
         scratch_shapes=[
-            pltpu.VMEM((PADDED, LANES), f32),
             pltpu.VMEM((PADDED, LANES), f32),
             pltpu.VMEM((LEV, LEV), f32),
             pltpu.VMEM((GROUPS, TAPS), f32),
             pltpu.VMEM((GROUPS, TAPS), f32),
             pltpu.VMEM((1, GROUPS), jnp.int32),
-            pltpu.VMEM((3, PADDED, LANES), f32),
-            pltpu.SemaphoreType.DMA((8,)),
+            pltpu.VMEM((2, 1, LANES), f32),
+            pltpu.SemaphoreType.DMA((7,)),
             pltpu.SemaphoreType.DMA((3,)),
             pltpu.VMEM((PADDED, LANES), f32),
             pltpu.VMEM((PADDED, LANES), f32),
@@ -445,6 +495,8 @@
             pltpu.VMEM((PADDED, PADDED), f32),
             pltpu.VMEM((2, 3, n_lat, chunk, LANES), f32),
             pltpu.VMEM((n_lat, chunk, LANES), f32),
+            pltpu.VMEM(side_shape, f32),
+            pltpu.VMEM(side_shape, f32),
             pltpu.VMEM((n_lat, 2, chunk, LANES), f32),
             pltpu.VMEM((TOGETHER, 2, STRIDE, 8, LANES), f32),
             pltpu.VMEM((TAPS, chunk, LANES), f32),
@@ -471,7 +523,6 @@
             vmem_limit_bytes=64 * 1024 * 1024,
         ),
     )(
-        iterate,
         residual,
         direction,
         obs_weight,
@@ -479,6 +530,12 @@
         lon_taps,
         lat_taps,
         band_sizes.reshape(1, GROUPS),
+    )
+    residual_next = residual - alpha * image
+    return (
+        iterate + alpha * direction,
+        residual_next,
+        residual_next + ratio * direction,
     )
 
 

time: 33.5 us -> 31.6 us (0.943)
  local copies, waits for them, and re-layouts: 2.98 us -> 0.66 us
  other arithmetic: 0 us -> 1.74 us
  Pallas kernels: 29.6 us -> 28.3 us
    unnamed x7 -> x4, local copies, waits for them, and re-layouts: 2.98 us -> 0.66 us
    add x0 -> x1, other arithmetic: none -> 1.74 us  [local(): residual_next + ratio * direction]
    pallas_call x1, Pallas kernels: 29.6 us -> 28.3 us  [local(): pl.pallas_call(functools.partial(kernel, n_lon, n_lat), out_shape=[jax.Sh...]
where the time goes in v3:
time: 31.6 us; the launch traced here: 31.4 us
  Pallas kernels  28.3 us (90%)
  other arithmetic  1.74 us (6%)
  local copies, waits for them, and re-layouts  0.66 us (2%)
  between operations  0.66 us (2%)
    pallas_call x1, Pallas kernels, local(): pl.pallas_call(functools.partial(kernel, n_lon, n_lat), out_shape=[jax.Sh...  28.3 us
    add x1, other arithmetic, local(): residual_next + ratio * direction  1.74 us
    unnamed x4, local copies, waits for them, and re-layouts  0.66 us

profile of v3, /device:TPU:0, one launch (start us, length us, event | category | flops | bytes accessed | tf_op | source)
XLA Modules:
  0.0 31.4 jit_solution(7223076228648019444)
XLA Ops:
  0.6 28.3 %shard_map.103 = (f32[127,1,128]{2,1,0:T(1,128)}, f32[1,1,128]{2,1,0:T(1,128)}, f32[1,1,128]{2,1,0:T(1,128)}) custom-call(f32[127,1,128]{2,1,0:T(1,128)} %residual_hbm.1, f32[127,1,128]{2,1,0:T(1,128)} %direction_hbm.1, f32[127,1,128]{2,1,0:T(1,128)} %weight_hbm.1, f32[127,127]{1,0:T(8,128)} %vertical_hbm.1, f32[32,101]{1,0:T(8,128)} %lon_taps_hbm.1, ...), custom_call_target="tpu_custom_call" | custom-call | tf_op jit(solution)/shard_map/pallas_call | solution.py:473
  29.0 0.0 copy-start
  29.0 0.0 copy-start.1
  29.0 0.6 %copy-done = f32[1,1,128]{2,1,0:T(1,128)S(1)} copy-done((f32[1,1,128]{2,1,0:T(1,128)S(1)}, f32[1,1,128]{2,1,0:T(1,128)}, u32[]{:S(2)}) %copy-start) | copy-done | bytes 536
  29.6 0.1 copy-done.1
  29.7 1.7 %multiply_add_fusion = (f32[127,1,128]{2,1,0:T(1,128)}, f32[127,1,128]{2,1,0:T(1,128)}, f32[127,1,128]{2,1,0:T(1,128)}) fusion(f32[127,1,128]{2,1,0:T(1,128)} %direction_hbm.1, f32[128]{0:T(128)S(1)} %bitcast.5, f32[127,1,128]{2,1,0:T(1,128)} %residual_hbm.1, f32[127,1,128]{2,1,0:T(1,128)} %get-tuple-element.7, f32[128]{0:T(128)S(1)} %bitcast.4, ...), kind=kLoop, calls=%fused_computation | loop fusion | flops 97536 | bytes 456192 | tf_op jit(solution)/shard_map/add | solution.py:538
Async XLA Ops:
  29.0 0.6 %copy-start = (f32[1,1,128]{2,1,0:T(1,128)S(1)}, f32[1,1,128]{2,1,0:T(1,128)}, u32[]{:S(2)}) copy-start(f32[1,1,128]{2,1,0:T(1,128)} %get-tuple-element.6) | copy-start | bytes 1540
  29.0 0.7 %copy-start.1 = (f32[1,1,128]{2,1,0:T(1,128)S(1)}, f32[1,1,128]{2,1,0:T(1,128)}, u32[]{:S(2)}) copy-start(f32[1,1,128]{2,1,0:T(1,128)} %get-tuple-element.8) | copy-start | bytes 1540

commit v4 on v3

--- a/solution.py
+++ b/solution.py
@@ -376,7 +376,6 @@
         sums[3] += total * total
 
     filter_chunk(1, True, add)
-    pending += send_back(image_part, image, 1)
 
     def exchange(slots, send, recv, mine, count, to_device, between=lambda: None):
         copies = []
@@ -413,6 +412,7 @@
     )
 
     def put_image():
+        pending.extend(send_back(image_part, image, 1))
         await_back(image, 1)
         store.start()
 

time: 31.6 us -> 31.6 us (level)
  no operation moved by 1% of the time
where the time goes in v4:
time: 31.6 us; the launch traced here: 31.4 us
  Pallas kernels  28.3 us (90%)
  other arithmetic  1.74 us (6%)
  local copies, waits for them, and re-layouts  0.66 us (2%)
  between operations  0.66 us (2%)
    pallas_call x1, Pallas kernels, local(): pl.pallas_call(functools.partial(kernel, n_lon, n_lat), out_shape=[jax.Sh...  28.3 us
    add x1, other arithmetic, local(): residual_next + ratio * direction  1.74 us
    unnamed x4, local copies, waits for them, and re-layouts  0.66 us

profile of v4, /device:TPU:0, one launch (start us, length us, event | category | flops | bytes accessed | tf_op | source)
XLA Modules:
  0.0 31.4 jit_solution(15681604103746393401)
XLA Ops:
  0.6 28.3 %shard_map.103 = (f32[127,1,128]{2,1,0:T(1,128)}, f32[1,1,128]{2,1,0:T(1,128)}, f32[1,1,128]{2,1,0:T(1,128)}) custom-call(f32[127,1,128]{2,1,0:T(1,128)} %residual_hbm.1, f32[127,1,128]{2,1,0:T(1,128)} %direction_hbm.1, f32[127,1,128]{2,1,0:T(1,128)} %weight_hbm.1, f32[127,127]{1,0:T(8,128)} %vertical_hbm.1, f32[32,101]{1,0:T(8,128)} %lon_taps_hbm.1, ...), custom_call_target="tpu_custom_call" | custom-call | tf_op jit(solution)/shard_map/pallas_call | solution.py:473
  29.0 0.0 copy-start
  29.0 0.0 copy-start.1
  29.0 0.6 %copy-done = f32[1,1,128]{2,1,0:T(1,128)S(1)} copy-done((f32[1,1,128]{2,1,0:T(1,128)S(1)}, f32[1,1,128]{2,1,0:T(1,128)}, u32[]{:S(2)}) %copy-start) | copy-done | bytes 536
  29.6 0.1 copy-done.1
  29.7 1.7 %multiply_add_fusion = (f32[127,1,128]{2,1,0:T(1,128)}, f32[127,1,128]{2,1,0:T(1,128)}, f32[127,1,128]{2,1,0:T(1,128)}) fusion(f32[127,1,128]{2,1,0:T(1,128)} %direction_hbm.1, f32[128]{0:T(128)S(1)} %bitcast.5, f32[127,1,128]{2,1,0:T(1,128)} %residual_hbm.1, f32[127,1,128]{2,1,0:T(1,128)} %get-tuple-element.7, f32[128]{0:T(128)S(1)} %bitcast.4, ...), kind=kLoop, calls=%fused_computation | loop fusion | flops 97536 | bytes 456192 | tf_op jit(solution)/shard_map/add | solution.py:538
Async XLA Ops:
  29.0 0.6 %copy-start = (f32[1,1,128]{2,1,0:T(1,128)S(1)}, f32[1,1,128]{2,1,0:T(1,128)}, u32[]{:S(2)}) copy-start(f32[1,1,128]{2,1,0:T(1,128)} %get-tuple-element.6) | copy-start | bytes 1540
  29.0 0.7 %copy-start.1 = (f32[1,1,128]{2,1,0:T(1,128)S(1)}, f32[1,1,128]{2,1,0:T(1,128)}, u32[]{:S(2)}) copy-start(f32[1,1,128]{2,1,0:T(1,128)} %get-tuple-element.8) | copy-start | bytes 1540
